TPU v7x, 128 devices: a whole 4x4x4 slice. The times are simulated.
128 devices in a mesh: wide: 8 (over y, core), col: 16 (over z, x).
Axes of the slice: x: 4, y: 4, z: 4, core: 2. Of those that a mesh axis runs over, the one named last changes fastest.
Arguments:
- rhs: float32 [98304, 256], P(('wide', 'col')), may hold values from -6 to 6
- basis: bfloat16 [98304, 256], P(('wide', 'col')), may hold values from -0.21875 to 0.21875
- self_block: bfloat16 [98304, 768], P(('wide', 'col'))
- near_block: bfloat16 [128, 8, 768, 768], P(('wide', 'col')), may hold values from -0.0546875 to 0.0546875
- near_ids: int32 [128, 8], P(('wide', 'col')), may hold values from -1 to 127, as said below
- couplings: bfloat16 [128, 40, 256, 256], P(('wide', 'col')), may hold values from -0.09375 to 0.09375
- far_ids: int32 [128, 40], P(('wide', 'col')), may hold values from -1 to 127, as said below
- intersection_start: int32 [128, 2], P(('wide', 'col')), may hold values from 0 to 512
- schwarz_inverse: bfloat16 [128, 1280, 1280], P(('wide', 'col'))
Outputs:
- solution: float32 [98304, 256], P(('wide', 'col'))
Inputs may be any that keep to these rules, and one draw needn't show every extreme that they name: `near_ids`: row c lists every cluster adjacent to cluster c on the grid (larger index distance 1; id = first index * 16 + second), ids first and -1 after them; rows of corner and edge clusters end in -1. `far_ids`: row c lists distinct clusters whose larger grid index distance from cluster c is 2 to 3, ids first and -1 after them; counts are ragged, and some rows list every such cluster. `intersection_start`: column 0 starts the rows taken by the domain of the cluster before along the second grid index, column 1 those taken by the one after.
All inputs are finite; a program needn't handle non-finite values.
Results may differ from a plain program's by a relative error of at most 0.0025.
The roundings to bfloat16 on the way count: a program that leaves them out, or rounds other values in their place, can miss the bound.
Values may be sent and summed in bfloat16 or wider, within the bound.
A program may use at most 128 MiB of HBM per device.

v0:
```python
import jax
import jax.numpy as jnp
from jax import lax
from jax.sharding import PartitionSpec as P

REACH = 3
ITERS = 2
HIGHEST_PREC = lax.Precision.HIGHEST
GROUP_SLOTS = 8


def passed_along(block, axis, distance):
    devices = range(lax.axis_size(axis))
    route = [(i - distance, i) for i in devices if i - distance in devices]
    return lax.ppermute(block, axis, route)


def with_halo(block, sides, width):
    for axis, dim in sides:
        count = lax.axis_size(axis)
        forward = [(i, i + 1) for i in range(count - 1)]
        backward = [(target, source) for source, target in forward]
        low = lax.ppermute(
            lax.slice_in_dim(block, block.shape[dim] - width, None, axis=dim), axis, forward
        )
        high = lax.ppermute(lax.slice_in_dim(block, 0, width, axis=dim), axis, backward)
        block = jnp.concatenate([low, block, high], axis=dim)
    return block


def local_gram(left, right):
    return lax.dot_general(
        left,
        right,
        (((0,), (0,)), ((), ())),
        precision=HIGHEST_PREC,
        preferred_element_type=jnp.float32,
    )


def lower_solve(factor, matrix):
    return lax.linalg.triangular_solve(
        factor, matrix, left_side=False, lower=True, transpose_a=True
    )


def far_window(coefficients):
    strip_row = jnp.stack(
        [
            coefficients if offset == 0 else passed_along(coefficients, "col", -offset)
            for offset in range(-REACH, REACH + 1)
        ]
    )
    window = jnp.stack(
        [
            strip_row if offset == 0 else passed_along(strip_row, "wide", -offset)
            for offset in range(-REACH, REACH + 1)
        ]
    )
    return window


def operate(vector_in, basis, self_block, near_block, near_ids, couplings, far_ids):
    rounded = vector_in.astype(jnp.bfloat16)
    cluster_rows, width = rounded.shape
    rank = basis.shape[1]
    wide_pos = lax.axis_index("wide")
    col_pos = lax.axis_index("col")
    col_count = lax.axis_size("col")
    result = jnp.dot(self_block, rounded, preferred_element_type=jnp.float32)
    beside_all = with_halo(rounded[None, None], (("wide", 0), ("col", 1)), 1)
    for slot_index in range(near_ids.shape[1]):
        neighbour = near_ids[0, slot_index]
        safe_id = jnp.maximum(neighbour, 0)
        wide_off = safe_id // col_count - wide_pos + 1
        col_off = safe_id % col_count - col_pos + 1
        other = lax.dynamic_slice(
            beside_all, (wide_off, col_off, 0, 0), (1, 1, cluster_rows, width)
        )[0, 0]
        product = jnp.dot(near_block[0, slot_index], other, preferred_element_type=jnp.float32)
        result = result + jnp.where(neighbour >= 0, product, jnp.zeros_like(product))
    coefficients = lax.dot_general(
        basis, rounded, (((0,), (0,)), ((), ())), preferred_element_type=jnp.float32
    ).astype(jnp.bfloat16)
    window = far_window(coefficients)
    span = 2 * REACH + 1
    flat_window = window.reshape(span * span, rank, width)
    far_list = far_ids[0]
    live_count = jnp.sum((far_list >= 0).astype(jnp.int32))
    group_count = (live_count + GROUP_SLOTS - 1) // GROUP_SLOTS

    def add_group(group_index, running):
        first_slot = group_index * GROUP_SLOTS
        targets = lax.dynamic_slice_in_dim(far_list, first_slot, GROUP_SLOTS, 0)
        safe_ids = jnp.maximum(targets, 0)
        flat_index = (safe_ids // col_count - wide_pos + REACH) * span + (
            safe_ids % col_count - col_pos + REACH
        )
        pieces_in = jnp.take(flat_window, flat_index, axis=0)
        coupling_group = lax.dynamic_slice_in_dim(couplings[0], first_slot, GROUP_SLOTS, 0)
        live_slots = (targets >= 0)[:, None, None]
        coupling_group = jnp.where(live_slots, coupling_group, jnp.zeros_like(coupling_group))
        return running + jnp.einsum(
            "lrs,lsk->rk", coupling_group, pieces_in, preferred_element_type=jnp.float32
        )

    far_sum = lax.fori_loop(0, group_count, add_group, jnp.zeros((rank, width), jnp.float32))
    return result + jnp.dot(basis, far_sum.astype(jnp.bfloat16), preferred_element_type=jnp.float32)


def add_rows(matrix, addend, start):
    current = lax.dynamic_slice_in_dim(matrix, start, addend.shape[0], 0)
    return lax.dynamic_update_slice_in_dim(matrix, current + addend, start, 0)


def precondition(vector_in, intersection_start, schwarz_inverse):
    rounded = vector_in.astype(jnp.bfloat16)
    cluster_rows = rounded.shape[0]
    margin = (schwarz_inverse.shape[1] - cluster_rows) // 2
    starts = intersection_start[0]
    prev_whole, prev_starts = passed_along((rounded, intersection_start), "col", 1)
    next_whole, next_starts = passed_along((rounded, intersection_start), "col", -1)
    prev_rows = lax.dynamic_slice_in_dim(prev_whole, prev_starts[0, 1], margin, 0)
    next_rows = lax.dynamic_slice_in_dim(next_whole, next_starts[0, 0], margin, 0)
    domain = jnp.concatenate([prev_rows, rounded, next_rows], axis=0)
    solved = jnp.dot(schwarz_inverse[0], domain, preferred_element_type=jnp.float32)
    result = solved[margin : margin + cluster_rows]
    from_next = passed_along(solved[:margin], "col", -1)
    from_prev = passed_along(solved[margin + cluster_rows :], "col", 1)
    result = add_rows(result, from_next, starts[1])
    result = add_rows(result, from_prev, starts[0])
    return result


def on_device(
    rhs,
    basis,
    self_block,
    near_block,
    near_ids,
    couplings,
    far_ids,
    intersection_start,
    schwarz_inverse,
):
    width = rhs.shape[1]
    first_sum = lax.psum(local_gram(rhs, rhs), ("wide", "col"))
    factor = jnp.linalg.cholesky(first_sum)
    beta_block = factor.T
    bases = [lower_solve(factor, rhs)]
    directions = []
    columns = []
    for iteration in range(ITERS):
        precond_out = precondition(bases[-1], intersection_start, schwarz_inverse)
        image = operate(precond_out, basis, self_block, near_block, near_ids, couplings, far_ids)
        stacked = jnp.concatenate(bases, axis=1)
        projected = lax.psum(local_gram(stacked, image), ("wide", "col"))
        image = image - jnp.dot(stacked, projected, precision=HIGHEST_PREC)
        gram_sum = lax.psum(local_gram(image, image), ("wide", "col"))
        factor = jnp.linalg.cholesky(gram_sum)
        columns.append((projected, factor.T))
        directions.append(precond_out)
        if iteration + 1 < ITERS:
            bases.append(lower_solve(factor, image))
    hessen = jnp.zeros(((ITERS + 1) * width, ITERS * width), jnp.float32)
    for column_index, (projected, sub_block) in enumerate(columns):
        upper_rows = (column_index + 1) * width
        hessen = hessen.at[:upper_rows, column_index * width : (column_index + 1) * width].set(
            projected
        )
        hessen = hessen.at[
            upper_rows : upper_rows + width, column_index * width : (column_index + 1) * width
        ].set(sub_block)
    normal_matrix = jnp.dot(hessen.T, hessen, precision=HIGHEST_PREC)
    target = jnp.dot(hessen[:width].T, beta_block, precision=HIGHEST_PREC)
    small_factor = jnp.linalg.cholesky(normal_matrix)
    middle = lax.linalg.triangular_solve(small_factor, target, left_side=True, lower=True)
    weights_y = lax.linalg.triangular_solve(
        small_factor, middle, left_side=True, lower=True, transpose_a=True
    )
    return jnp.dot(jnp.concatenate(directions, axis=1), weights_y, precision=HIGHEST_PREC)


def solution(mesh):
    in_specs = (
        P(("wide", "col"), None),
        P(("wide", "col"), None),
        P(("wide", "col"), None),
        P(("wide", "col"), None, None, None),
        P(("wide", "col"), None),
        P(("wide", "col"), None, None, None),
        P(("wide", "col"), None),
        P(("wide", "col"), None),
        P(("wide", "col"), None, None),
    )
    out_specs = P(("wide", "col"), None)
    return jax.shard_map(
        on_device, mesh=mesh, in_specs=in_specs, out_specs=out_specs, check_vma=False
    )
```

profile of v0, /device:TPU:1, one launch (start us, length us, event | category | flops | bytes accessed | tf_op | source)
XLA Modules:
  0.0 1556.4 jit_solution(12817224653365156530)
XLA Ops:
  10.3 146.7 %all-reduce.9.cloned.1.call-done = f32[256,256]{0,1:T(8,128)} async-done(((f32[256,256]{0,1:T(8,128)}), f32[256,256]{0,1:T(8,128)}) %all-reduce.9.cloned.1.call-update) | async-done | bytes 262160 | tf_op jit(solution)/shard_map/psum | solution.py:147
  159.7 11.7 cholesky.392
  172.1 10.4 custom-call.47
  186.2 13.2 cholesky.402
  211.1 21.1 %custom-call.48 = f32[2,128,128]{1,2,0:T(8,128)} custom-call(f32[2,128,128]{2,1,0:T(8,128)} %get-tuple-element.295), custom_call_target="InvertDiagBlocksLowerTriangular" | custom-call | tf_op jit(solution)/shard_map/triangular_solve/custom-call.9 | solution.py:42
  339.1 19.0 %collective-permute-done.6 = bf16[1,1,768,256]{2,3,1,0:T(8,128)(2,1)} collective-permute-done((bf16[1,1,768,256]{2,3,1,0:T(8,128)(2,1)}, bf16[1,1,768,256]{2,3,1,0:T(8,128)(2,1)}, u32[]{:S(2)}, u32[]{:S(2)}) %collective-permute-start.6) | collective-permute-done | bytes 393248 | tf_op jit(solution)/shard_map/ppermute | solution.py:23
  387.8 9.3 copy.13
  397.9 14.7 while.33
  428.6 185.3 %all-reduce.11.cloned.1.call-done = f32[256,256]{1,0:T(8,128)} async-done(((f32[256,256]{1,0:T(8,128)}), f32[256,256]{1,0:T(8,128)}) %all-reduce.11.cloned.1.call-update) | async-done | bytes 262160 | tf_op jit(solution)/shard_map/psum | solution.py:157
  618.9 138.9 %all-reduce.13.cloned.1.call-done = f32[256,256]{0,1:T(8,128)} async-done(((f32[256,256]{0,1:T(8,128)}), f32[256,256]{0,1:T(8,128)}) %all-reduce.13.cloned.1.call-update) | async-done | bytes 262160 | tf_op jit(solution)/shard_map/psum | solution.py:159
  762.0 13.2 cholesky.419
  778.2 11.3 custom-call.49
  792.9 13.2 cholesky.429
  820.2 21.1 %custom-call.50 = f32[2,128,128]{1,2,0:T(8,128)} custom-call(f32[2,128,128]{2,1,0:T(8,128)} %get-tuple-element.296), custom_call_target="InvertDiagBlocksLowerTriangular" | custom-call | tf_op jit(solution)/shard_map/triangular_solve/custom-call.9 | solution.py:42
  875.1 9.7 collective-permute-start.30
  922.9 30.5 %collective-permute-done.26 = bf16[1,1,768,256]{2,3,1,0:T(8,128)(2,1)S(1)} collective-permute-done((bf16[1,1,768,256]{2,3,1,0:T(8,128)(2,1)S(1)}, bf16[1,1,768,256]{2,3,1,0:T(8,128)(2,1)S(1)}, u32[]{:S(2)}, u32[]{:S(2)}) %collective-permute-start.26) | collective-permute-done | bytes 393248 | tf_op jit(solution)/shard_map/ppermute | solution.py:23
  983.0 9.3 copy.19
  993.1 12.1 while.34
  1023.1 184.5 %all-reduce.15.cloned.1.call-done = f32[512,256]{1,0:T(8,128)} async-done(((f32[512,256]{1,0:T(8,128)}), f32[512,256]{1,0:T(8,128)}) %all-reduce.15.cloned.1.call-update) | async-done | bytes 524304 | tf_op jit(solution)/shard_map/psum | solution.py:157
  1221.8 131.3 %all-reduce.17.cloned.1.call-done = f32[256,256]{0,1:T(8,128)} async-done(((f32[256,256]{0,1:T(8,128)}), f32[256,256]{0,1:T(8,128)}) %all-reduce.17.cloned.1.call-update) | async-done | bytes 262160 | tf_op jit(solution)/shard_map/psum | solution.py:159
  1355.2 11.7 cholesky.446
  1367.0 9.8 custom-call.51
  1377.2 11.7 cholesky.456
  1397.7 11.7 cholesky.167
  1409.5 9.8 custom-call.37
  1421.9 11.9 cholesky.190
  1435.1 9.8 custom-call.38
  1446.5 11.7 cholesky.294
  1459.0 9.8 custom-call.52
  1470.2 11.9 cholesky.307
  1485.6 10.6 while.35
  1496.2 40.2 %custom-call.39 = f32[4,128,128]{1,2,0:T(8,128)S(1)} custom-call(f32[4,128,128]{2,1,0:T(8,128)} %get-tuple-element.288), custom_call_target="InvertDiagBlocksLowerTriangular" | custom-call | tf_op jit(solution)/shard_map/triangular_solve | solution.py:178
  (407 shorter events, 402.9 us)
Async XLA Ops:
  6.5 150.4 %all-reduce.9.cloned.1.call-start = ((), (), s32[]{:S(2)}) async-start(), calls=%async_computation | async-start | bytes 524288 | tf_op jit(solution)/shard_map/psum | solution.py:147
  10.2 603.7 %all-reduce.11.cloned.1.call-start = ((), (), s32[]{:S(2)}) async-start(), calls=%async_computation.1 | async-start | bytes 524288 | tf_op jit(solution)/shard_map/psum | solution.py:157
  238.0 15.6 %collective-permute-start = (bf16[768,256]{0,1:T(8,128)(2,1)}, bf16[768,256]{0,1:T(8,128)(2,1)}, u32[]{:S(2)}, u32[]{:S(2)}) collective-permute-start(bf16[768,256]{0,1:T(8,128)(2,1)} %fusion.109), channel_id=1, source_target_pairs={{0,1},{1,2},{2,3},{3,4},{4,5},{5,6},{6,7},{7,8},{8,9},{9,10},{10,1... | collective-permute-start | bytes 1179656 | tf_op jit(solution)/shard_map/ppermute | solution.py:15
  241.4 13.3 collective-permute-start.2
  260.9 14.9 collective-permute-start.5
  281.5 15.3 collective-permute-start.10
  296.8 12.0 collective-permute-start.15
  309.5 54.3 %collective-permute-start.16 = (bf16[7,256,256]{1,2,0:T(8,128)(2,1)}, bf16[7,256,256]{1,2,0:T(8,128)(2,1)}, u32[]{:S(2)}, u32[]{:S(2)}) collective-permute-start(bf16[7,256,256]{1,2,0:T(8,128)(2,1)} %bitcast_dynamic-update-slice_fusion.25), channel_id=1, source_target_pairs={{0,48},{16,64},{32,80},{48,96},{64,112},{1,49},{17,65},{33,81},{49... | collective-permute-start | bytes 2752520 | tf_op jit(solution)/shard_map/ppermute | solution.py:15
  316.5 50.7 %collective-permute-start.17 = (bf16[7,256,256]{1,2,0:T(8,128)(2,1)}, bf16[7,256,256]{1,2,0:T(8,128)(2,1)}, u32[]{:S(2)}, u32[]{:S(2)}) collective-permute-start(bf16[7,256,256]{1,2,0:T(8,128)(2,1)} %bitcast_dynamic-update-slice_fusion.25), channel_id=1, source_target_pairs={{0,32},{16,48},{32,64},{48,80},{64,96},{80,112},{1,33},{17,49},{33... | collective-permute-start | bytes 2752520 | tf_op jit(solution)/shard_map/ppermute | solution.py:15
  319.5 38.6 %collective-permute-start.6 = (bf16[1,1,768,256]{2,3,1,0:T(8,128)(2,1)}, bf16[1,1,768,256]{2,3,1,0:T(8,128)(2,1)}, u32[]{:S(2)}, u32[]{:S(2)}) collective-permute-start(bf16[1,1,768,256]{2,3,1,0:T(8,128)(2,1)} %convert_bitcast_fusion.1), channel_id=1, source_target_pairs={{0,16},{16,32},{32,48},{48,64},{64,80},{80,96},{96,112},{1,17},{17... | collective-permute-start | bytes 1179656 | tf_op jit(solution)/shard_map/ppermute | solution.py:23
  321.5 38.6 %collective-permute-start.7 = (bf16[1,1,768,256]{2,3,1,0:T(8,128)(2,1)}, bf16[1,1,768,256]{2,3,1,0:T(8,128)(2,1)}, u32[]{:S(2)}, u32[]{:S(2)}) collective-permute-start(bf16[1,1,768,256]{2,3,1,0:T(8,128)(2,1)} %convert_bitcast_fusion.1), channel_id=1, source_target_pairs={{16,0},{32,16},{48,32},{64,48},{80,64},{96,80},{112,96},{17,1},{33... | collective-permute-start | bytes 1179656 | tf_op jit(solution)/shard_map/ppermute | solution.py:26
  324.6 49.8 %collective-permute-start.18 = (bf16[7,256,256]{1,2,0:T(8,128)(2,1)}, bf16[7,256,256]{1,2,0:T(8,128)(2,1)}, u32[]{:S(2)}, u32[]{:S(2)}) collective-permute-start(bf16[7,256,256]{1,2,0:T(8,128)(2,1)} %bitcast_dynamic-update-slice_fusion.25), channel_id=1, source_target_pairs={{0,16},{16,32},{32,48},{48,64},{64,80},{80,96},{96,112},{1,17},{17... | collective-permute-start | bytes 2752520 | tf_op jit(solution)/shard_map/ppermute | solution.py:15
  358.2 23.7 %collective-permute-start.19 = (bf16[7,256,256]{1,2,0:T(8,128)(2,1)}, bf16[7,256,256]{1,2,0:T(8,128)(2,1)S(1)}, u32[]{:S(2)}, u32[]{:S(2)}) collective-permute-start(bf16[7,256,256]{1,2,0:T(8,128)(2,1)} %bitcast_dynamic-update-slice_fusion.25), channel_id=1, source_target_pairs={{16,0},{32,16},{48,32},{64,48},{80,64},{96,80},{112,96},{17,1},{33... | collective-permute-start | bytes 2752520 | tf_op jit(solution)/shard_map/ppermute | solution.py:15
  360.1 25.7 %collective-permute-start.20 = (bf16[7,256,256]{1,2,0:T(8,128)(2,1)}, bf16[7,256,256]{1,2,0:T(8,128)(2,1)S(1)}, u32[]{:S(2)}, u32[]{:S(2)}) collective-permute-start(bf16[7,256,256]{1,2,0:T(8,128)(2,1)} %bitcast_dynamic-update-slice_fusion.25), channel_id=1, source_target_pairs={{32,0},{48,16},{64,32},{80,48},{96,64},{112,80},{33,1},{49,17},{65... | collective-permute-start | bytes 2752520 | tf_op jit(solution)/shard_map/ppermute | solution.py:15
  363.8 23.0 %collective-permute-start.21 = (bf16[7,256,256]{1,2,0:T(8,128)(2,1)}, bf16[7,256,256]{1,2,0:T(8,128)(2,1)S(1)}, u32[]{:S(2)}, u32[]{:S(2)}) collective-permute-start(bf16[7,256,256]{1,2,0:T(8,128)(2,1)} %bitcast_dynamic-update-slice_fusion.25), channel_id=1, source_target_pairs={{48,0},{64,16},{80,32},{96,48},{112,64},{49,1},{65,17},{81,33},{97... | collective-permute-start | bytes 2752520 | tf_op jit(solution)/shard_map/ppermute | solution.py:15
  367.2 45.4 %collective-permute-start.8 = (bf16[3,1,768,256]{2,3,1,0:T(8,128)(2,1)}, bf16[3,1,768,256]{2,3,1,0:T(8,128)(2,1)}, u32[]{:S(2)}, u32[]{:S(2)}) collective-permute-start(bf16[3,1,768,256]{2,3,1,0:T(8,128)(2,1)} %pad_maximum_fusion.2), channel_id=1, source_target_pairs={{0,1},{1,2},{2,3},{3,4},{4,5},{5,6},{6,7},{7,8},{8,9},{9,10},{10,1... | collective-permute-start | bytes 3538952 | tf_op jit(solution)/shard_map/ppermute | solution.py:23
  374.4 38.2 %collective-permute-start.9 = (bf16[3,1,768,256]{2,3,1,0:T(8,128)(2,1)}, bf16[3,1,768,256]{2,3,1,0:T(8,128)(2,1)}, u32[]{:S(2)}, u32[]{:S(2)}) collective-permute-start(bf16[3,1,768,256]{2,3,1,0:T(8,128)(2,1)} %pad_maximum_fusion.2), channel_id=1, source_target_pairs={{1,0},{2,1},{3,2},{4,3},{5,4},{6,5},{7,6},{8,7},{9,8},{10,9},{11,1... | collective-permute-start | bytes 3538952 | tf_op jit(solution)/shard_map/ppermute | solution.py:26
  428.5 329.3 %all-reduce.13.cloned.1.call-start = ((), (), s32[]{:S(2)}) async-start(), calls=%async_computation.2 | async-start | bytes 524288 | tf_op jit(solution)/shard_map/psum | solution.py:159
  618.6 589.0 %all-reduce.15.cloned.1.call-start = ((), (), s32[]{:S(2)}) async-start(), calls=%async_computation.3 | async-start | bytes 1048576 | tf_op jit(solution)/shard_map/psum | solution.py:157
  875.1 16.7 %collective-permute-start.30 = (bf16[256,256]{0,1:T(8,128)(2,1)S(1)}, bf16[256,256]{0,1:T(8,128)(2,1)S(1)}, u32[]{:S(2)}, u32[]{:S(2)}) collective-permute-start(bf16[256,256]{0,1:T(8,128)(2,1)S(1)} %bitcast.418), channel_id=1, source_target_pairs={{0,3},{1,4},{2,5},{3,6},{4,7},{5,8},{6,9},{7,10},{8,11},{9,12},{10... | collective-permute-start | bytes 393224 | tf_op jit(solution)/shard_map/ppermute | solution.py:15
  891.8 12.3 collective-permute-start.35
  904.8 52.9 %collective-permute-start.36 = (bf16[7,256,256]{1,2,0:T(8,128)(2,1)}, bf16[7,256,256]{1,2,0:T(8,128)(2,1)}, u32[]{:S(2)}, u32[]{:S(2)}) collective-permute-start(bf16[7,256,256]{1,2,0:T(8,128)(2,1)} %bitcast_dynamic-update-slice_fusion.19), channel_id=1, source_target_pairs={{0,48},{16,64},{32,80},{48,96},{64,112},{1,49},{17,65},{33,81},{49... | collective-permute-start | bytes 2752520 | tf_op jit(solution)/shard_map/ppermute | solution.py:15
  913.1 48.1 %collective-permute-start.37 = (bf16[7,256,256]{1,2,0:T(8,128)(2,1)}, bf16[7,256,256]{1,2,0:T(8,128)(2,1)}, u32[]{:S(2)}, u32[]{:S(2)}) collective-permute-start(bf16[7,256,256]{1,2,0:T(8,128)(2,1)} %bitcast_dynamic-update-slice_fusion.19), channel_id=1, source_target_pairs={{0,32},{16,48},{32,64},{48,80},{64,96},{80,112},{1,33},{17,49},{33... | collective-permute-start | bytes 2752520 | tf_op jit(solution)/shard_map/ppermute | solution.py:15
  915.3 38.0 %collective-permute-start.26 = (bf16[1,1,768,256]{2,3,1,0:T(8,128)(2,1)S(1)}, bf16[1,1,768,256]{2,3,1,0:T(8,128)(2,1)S(1)}, u32[]{:S(2)}, u32[]{:S(2)}) collective-permute-start(bf16[1,1,768,256]{2,3,1,0:T(8,128)(2,1)S(1)} %convert_bitcast_fusion), channel_id=1, source_target_pairs={{0,16},{16,32},{32,48},{48,64},{64,80},{80,96},{96,112},{1,17},{17... | collective-permute-start | bytes 1179656 | tf_op jit(solution)/shard_map/ppermute | solution.py:23
  917.3 38.0 %collective-permute-start.27 = (bf16[1,1,768,256]{2,3,1,0:T(8,128)(2,1)S(1)}, bf16[1,1,768,256]{2,3,1,0:T(8,128)(2,1)S(1)}, u32[]{:S(2)}, u32[]{:S(2)}) collective-permute-start(bf16[1,1,768,256]{2,3,1,0:T(8,128)(2,1)S(1)} %convert_bitcast_fusion), channel_id=1, source_target_pairs={{16,0},{32,16},{48,32},{64,48},{80,64},{96,80},{112,96},{17,1},{33... | collective-permute-start | bytes 1179656 | tf_op jit(solution)/shard_map/ppermute | solution.py:26
  919.7 48.7 %collective-permute-start.38 = (bf16[7,256,256]{1,2,0:T(8,128)(2,1)}, bf16[7,256,256]{1,2,0:T(8,128)(2,1)}, u32[]{:S(2)}, u32[]{:S(2)}) collective-permute-start(bf16[7,256,256]{1,2,0:T(8,128)(2,1)} %bitcast_dynamic-update-slice_fusion.19), channel_id=1, source_target_pairs={{0,16},{16,32},{32,48},{48,64},{64,80},{80,96},{96,112},{1,17},{17... | collective-permute-start | bytes 2752520 | tf_op jit(solution)/shard_map/ppermute | solution.py:15
  953.3 23.7 %collective-permute-start.39 = (bf16[7,256,256]{1,2,0:T(8,128)(2,1)}, bf16[7,256,256]{1,2,0:T(8,128)(2,1)S(1)}, u32[]{:S(2)}, u32[]{:S(2)}) collective-permute-start(bf16[7,256,256]{1,2,0:T(8,128)(2,1)} %bitcast_dynamic-update-slice_fusion.19), channel_id=1, source_target_pairs={{16,0},{32,16},{48,32},{64,48},{80,64},{96,80},{112,96},{17,1},{33... | collective-permute-start | bytes 2752520 | tf_op jit(solution)/shard_map/ppermute | solution.py:15
  955.3 25.7 %collective-permute-start.40 = (bf16[7,256,256]{1,2,0:T(8,128)(2,1)}, bf16[7,256,256]{1,2,0:T(8,128)(2,1)S(1)}, u32[]{:S(2)}, u32[]{:S(2)}) collective-permute-start(bf16[7,256,256]{1,2,0:T(8,128)(2,1)} %bitcast_dynamic-update-slice_fusion.19), channel_id=1, source_target_pairs={{32,0},{48,16},{64,32},{80,48},{96,64},{112,80},{33,1},{49,17},{65... | collective-permute-start | bytes 2752520 | tf_op jit(solution)/shard_map/ppermute | solution.py:15
  957.7 24.2 %collective-permute-start.41 = (bf16[7,256,256]{1,2,0:T(8,128)(2,1)}, bf16[7,256,256]{1,2,0:T(8,128)(2,1)S(1)}, u32[]{:S(2)}, u32[]{:S(2)}) collective-permute-start(bf16[7,256,256]{1,2,0:T(8,128)(2,1)} %bitcast_dynamic-update-slice_fusion.19), channel_id=1, source_target_pairs={{48,0},{64,16},{80,32},{96,48},{112,64},{49,1},{65,17},{81,33},{97... | collective-permute-start | bytes 2752520 | tf_op jit(solution)/shard_map/ppermute | solution.py:15
  961.2 44.0 %collective-permute-start.28 = (bf16[3,1,768,256]{2,3,1,0:T(8,128)(2,1)}, bf16[3,1,768,256]{2,3,1,0:T(8,128)(2,1)}, u32[]{:S(2)}, u32[]{:S(2)}) collective-permute-start(bf16[3,1,768,256]{2,3,1,0:T(8,128)(2,1)} %pad_maximum_fusion.3), channel_id=1, source_target_pairs={{0,1},{1,2},{2,3},{3,4},{4,5},{5,6},{6,7},{7,8},{8,9},{9,10},{10,1... | collective-permute-start | bytes 3538952 | tf_op jit(solution)/shard_map/ppermute | solution.py:23
  968.4 36.7 %collective-permute-start.29 = (bf16[3,1,768,256]{2,3,1,0:T(8,128)(2,1)}, bf16[3,1,768,256]{2,3,1,0:T(8,128)(2,1)}, u32[]{:S(2)}, u32[]{:S(2)}) collective-permute-start(bf16[3,1,768,256]{2,3,1,0:T(8,128)(2,1)} %pad_maximum_fusion.3), channel_id=1, source_target_pairs={{1,0},{2,1},{3,2},{4,3},{5,4},{6,5},{7,6},{8,7},{9,8},{10,9},{11,1... | collective-permute-start | bytes 3538952 | tf_op jit(solution)/shard_map/ppermute | solution.py:26
  1020.4 332.6 %all-reduce.17.cloned.1.call-start = ((), (), s32[]{:S(2)}) async-start(), calls=%async_computation.4 | async-start | bytes 524288 | tf_op jit(solution)/shard_map/psum | solution.py:159
  (60 other events, 1485.7 us)
Sparse Core Ops, SparseCore 0:
  12.1 144.7 all-reduce.8
  428.6 185.2 all-reduce.10
  618.8 138.9 all-reduce.12
  1020.6 186.9 all-reduce.14
  1212.9 140.1 all-reduce.16
where the time goes:
time: 1570 us; the launch traced here: 1560 us
  waiting for transfers between devices  876 us (56%)
  other arithmetic  300 us (19%)
  local copies, waits for them, and re-layouts  133 us (8%)
  starting transfers between devices  117 us (7%)
  matrix products  91.5 us (6%)
  between operations  37.7 us (2%)
    psum x2, waiting for transfers between devices, on_device(): projected = lax.psum(local_gram(stacked, image), ('wide', 'col'))  370 us
    psum x2, waiting for transfers between devices, on_device(): gram_sum = lax.psum(local_gram(image, image), ('wide', 'col'))  270 us
    psum x1, waiting for transfers between devices, on_device(): first_sum = lax.psum(local_gram(rhs, rhs), ('wide', 'col'))  147 us
    ppermute x34, starting transfers between devices, passed_along(): return lax.ppermute(block, axis, route)  94.5 us
    another operation x15, other arithmetic, on_device(): small_factor = jnp.linalg.cholesky(normal_matrix)  79.5 us
    another operation x14, other arithmetic, on_device(): factor = jnp.linalg.cholesky(gram_sum)  76.6 us
    ppermute x4, waiting for transfers between devices, with_halo(): lax.ppermute(lax.slice_in_dim(block, block.shape[dim] - width, None, axis...  49.5 us
    another operation x4, other arithmetic, lower_solve(): lax.linalg.triangular_solve(factor, matrix, left_side=False, lower=True,...  42.9 us
  transfers between devices with their start and end apart: 47, of which 22 were waited for; matrix products, arithmetic and copies ran while one was open for 7% of the time, Pallas kernels for 0%

commit v1 on v0

--- a/solution.py
+++ b/solution.py
@@ -144,7 +144,8 @@
     schwarz_inverse,
 ):
     width = rhs.shape[1]
-    first_sum = lax.psum(local_gram(rhs, rhs), ("wide", "col"))
+    s0 = local_gram(rhs, rhs)
+    first_sum = jax.lax.all_gather(s0, axis_name=("wide", "col")).sum(axis=0)
     factor = jnp.linalg.cholesky(first_sum)
     beta_block = factor.T
     bases = [lower_solve(factor, rhs)]

time: 1570 us -> 1550 us (0.987)
  waiting for transfers between devices: 876 us -> 841 us
    psum x1 -> x0, waiting for transfers between devices: 147 us -> none  [on_device(): first_sum = lax.psum(local_gram(rhs, rhs), ('wide', 'col'))]
    all_gather x0 -> x1, waiting for transfers between devices: none -> 111 us  [on_device(): first_sum = jax.lax.all_gather(s0, axis_name=('wide', 'col')).sum(axis=0)]
where the time goes in v1:
time: 1550 us; the launch traced here: 1530 us
  waiting for transfers between devices  841 us (54%)
  other arithmetic  313 us (20%)
  local copies, waits for them, and re-layouts  133 us (9%)
  starting transfers between devices  116 us (7%)
  matrix products  91.5 us (6%)
  between operations  37.6 us (2%)
    psum x2, waiting for transfers between devices, on_device(): projected = lax.psum(local_gram(stacked, image), ('wide', 'col'))  371 us
    psum x2, waiting for transfers between devices, on_device(): gram_sum = lax.psum(local_gram(image, image), ('wide', 'col'))  270 us
    all_gather x1, waiting for transfers between devices, on_device(): first_sum = jax.lax.all_gather(s0, axis_name=('wide', 'col')).sum(axis=0)  111 us
    ppermute x34, starting transfers between devices, passed_along(): return lax.ppermute(block, axis, route)  93.9 us
    another operation x15, other arithmetic, on_device(): small_factor = jnp.linalg.cholesky(normal_matrix)  79.5 us
    another operation x14, other arithmetic, on_device(): factor = jnp.linalg.cholesky(gram_sum)  76.6 us
    ppermute x4, waiting for transfers between devices, with_halo(): lax.ppermute(lax.slice_in_dim(block, block.shape[dim] - width, None, axis...  48.1 us
    another operation x4, other arithmetic, lower_solve(): lax.linalg.triangular_solve(factor, matrix, left_side=False, lower=True,...  43.4 us
  transfers between devices with their start and end apart: 47, of which 22 were waited for; matrix products, arithmetic and copies ran while one was open for 7% of the time, Pallas kernels for 0%

profile of v1, /device:TPU:1, one launch (start us, length us, event | category | flops | bytes accessed | tf_op | source)
XLA Modules:
  0.0 1532.5 jit_solution(8782767550591774725)
XLA Ops:
  10.3 110.6 %all-gather.3.cloned.1.call-done = f32[32768,256]{1,0:T(8,128)} async-done(((f32[256,256]{1,0:T(8,128)}), f32[32768,256]{1,0:T(8,128)}) %all-gather.3.cloned.1.call-update) | async-done | bytes 33554448 | tf_op jit(solution)/shard_map/all_gather | solution.py:148
  120.9 12.0 reduce_sum.16
  135.4 11.7 cholesky.392
  147.8 10.4 custom-call.47
  161.9 13.2 cholesky.402
  186.3 21.5 %custom-call.48 = f32[2,128,128]{1,2,0:T(8,128)} custom-call(f32[2,128,128]{2,1,0:T(8,128)} %get-tuple-element.295), custom_call_target="InvertDiagBlocksLowerTriangular" | custom-call | tf_op jit(solution)/shard_map/triangular_solve/custom-call.9 | solution.py:42
  315.4 17.6 %collective-permute-done.6 = bf16[1,1,768,256]{2,3,1,0:T(8,128)(2,1)} collective-permute-done((bf16[1,1,768,256]{2,3,1,0:T(8,128)(2,1)}, bf16[1,1,768,256]{2,3,1,0:T(8,128)(2,1)}, u32[]{:S(2)}, u32[]{:S(2)}) %collective-permute-start.6) | collective-permute-done | bytes 393248 | tf_op jit(solution)/shard_map/ppermute | solution.py:23
  362.7 9.3 copy.27
  372.7 14.7 while.33
  403.4 186.8 %all-reduce.8.cloned.1.call-done = f32[256,256]{1,0:T(8,128)} async-done(((f32[256,256]{1,0:T(8,128)}), f32[256,256]{1,0:T(8,128)}) %all-reduce.8.cloned.1.call-update) | async-done | bytes 262160 | tf_op jit(solution)/shard_map/psum | solution.py:158
  595.2 138.9 %all-reduce.10.cloned.1.call-done = f32[256,256]{0,1:T(8,128)} async-done(((f32[256,256]{0,1:T(8,128)}), f32[256,256]{0,1:T(8,128)}) %all-reduce.10.cloned.1.call-update) | async-done | bytes 262160 | tf_op jit(solution)/shard_map/psum | solution.py:160
  738.3 13.2 cholesky.419
  754.5 11.3 custom-call.49
  769.2 13.2 cholesky.429
  796.5 21.1 %custom-call.50 = f32[2,128,128]{1,2,0:T(8,128)} custom-call(f32[2,128,128]{2,1,0:T(8,128)} %get-tuple-element.296), custom_call_target="InvertDiagBlocksLowerTriangular" | custom-call | tf_op jit(solution)/shard_map/triangular_solve/custom-call.9 | solution.py:42
  851.4 9.7 collective-permute-start.30
  899.1 30.5 %collective-permute-done.26 = bf16[1,1,768,256]{2,3,1,0:T(8,128)(2,1)S(1)} collective-permute-done((bf16[1,1,768,256]{2,3,1,0:T(8,128)(2,1)S(1)}, bf16[1,1,768,256]{2,3,1,0:T(8,128)(2,1)S(1)}, u32[]{:S(2)}, u32[]{:S(2)}) %collective-permute-start.26) | collective-permute-done | bytes 393248 | tf_op jit(solution)/shard_map/ppermute | solution.py:23
  969.3 12.1 while.34
  999.5 184.4 %all-reduce.12.cloned.1.call-done = f32[512,256]{1,0:T(8,128)} async-done(((f32[512,256]{1,0:T(8,128)}), f32[512,256]{1,0:T(8,128)}) %all-reduce.12.cloned.1.call-update) | async-done | bytes 524304 | tf_op jit(solution)/shard_map/psum | solution.py:158
  1197.9 131.4 %all-reduce.14.cloned.1.call-done = f32[256,256]{0,1:T(8,128)} async-done(((f32[256,256]{0,1:T(8,128)}), f32[256,256]{0,1:T(8,128)}) %all-reduce.14.cloned.1.call-update) | async-done | bytes 262160 | tf_op jit(solution)/shard_map/psum | solution.py:160
  1331.4 11.7 cholesky.446
  1343.2 9.8 custom-call.51
  1353.5 11.7 cholesky.456
  1373.9 11.7 cholesky.167
  1385.8 9.8 custom-call.37
  1398.1 11.9 cholesky.190
  1411.4 9.8 custom-call.38
  1422.8 11.7 cholesky.294
  1435.2 9.8 custom-call.52
  1446.4 11.9 cholesky.307
  1461.7 10.6 while.35
  1472.3 40.2 %custom-call.39 = f32[4,128,128]{1,2,0:T(8,128)S(1)} custom-call(f32[4,128,128]{2,1,0:T(8,128)} %get-tuple-element.288), custom_call_target="InvertDiagBlocksLowerTriangular" | custom-call | tf_op jit(solution)/shard_map/triangular_solve | solution.py:179
  (408 shorter events, 412.0 us)
Async XLA Ops:
  6.5 114.4 %all-gather.3.cloned.1.call-start = ((), (), s32[]{:S(2)}) async-start(), calls=%async_computation.4 | async-start | bytes 33816576 | tf_op jit(solution)/shard_map/all_gather | solution.py:148
  10.2 580.0 %all-reduce.8.cloned.1.call-start = ((), (), s32[]{:S(2)}) async-start(), calls=%async_computation | async-start | bytes 524288 | tf_op jit(solution)/shard_map/psum | solution.py:158
  213.6 17.0 %collective-permute-start = (bf16[768,256]{0,1:T(8,128)(2,1)}, bf16[768,256]{0,1:T(8,128)(2,1)}, u32[]{:S(2)}, u32[]{:S(2)}) collective-permute-start(bf16[768,256]{0,1:T(8,128)(2,1)} %fusion.109), channel_id=1, source_target_pairs={{0,1},{1,2},{2,3},{3,4},{4,5},{5,6},{6,7},{7,8},{8,9},{9,10},{10,1... | collective-permute-start | bytes 1179656 | tf_op jit(solution)/shard_map/ppermute | solution.py:15
  217.5 14.1 collective-permute-start.2
  238.0 14.9 collective-permute-start.5
  258.5 13.1 collective-permute-start.10
  271.6 12.3 collective-permute-start.15
  284.6 54.0 %collective-permute-start.16 = (bf16[7,256,256]{1,2,0:T(8,128)(2,1)}, bf16[7,256,256]{1,2,0:T(8,128)(2,1)}, u32[]{:S(2)}, u32[]{:S(2)}) collective-permute-start(bf16[7,256,256]{1,2,0:T(8,128)(2,1)} %bitcast_dynamic-update-slice_fusion.25), channel_id=1, source_target_pairs={{0,48},{16,64},{32,80},{48,96},{64,112},{1,49},{17,65},{33,81},{49... | collective-permute-start | bytes 2752520 | tf_op jit(solution)/shard_map/ppermute | solution.py:15
  292.8 49.3 %collective-permute-start.17 = (bf16[7,256,256]{1,2,0:T(8,128)(2,1)}, bf16[7,256,256]{1,2,0:T(8,128)(2,1)}, u32[]{:S(2)}, u32[]{:S(2)}) collective-permute-start(bf16[7,256,256]{1,2,0:T(8,128)(2,1)} %bitcast_dynamic-update-slice_fusion.25), channel_id=1, source_target_pairs={{0,32},{16,48},{32,64},{48,80},{64,96},{80,112},{1,33},{17,49},{33... | collective-permute-start | bytes 2752520 | tf_op jit(solution)/shard_map/ppermute | solution.py:15
  295.8 37.2 %collective-permute-start.6 = (bf16[1,1,768,256]{2,3,1,0:T(8,128)(2,1)}, bf16[1,1,768,256]{2,3,1,0:T(8,128)(2,1)}, u32[]{:S(2)}, u32[]{:S(2)}) collective-permute-start(bf16[1,1,768,256]{2,3,1,0:T(8,128)(2,1)} %convert_bitcast_fusion.1), channel_id=1, source_target_pairs={{0,16},{16,32},{32,48},{48,64},{64,80},{80,96},{96,112},{1,17},{17... | collective-permute-start | bytes 1179656 | tf_op jit(solution)/shard_map/ppermute | solution.py:23
  297.7 37.2 %collective-permute-start.7 = (bf16[1,1,768,256]{2,3,1,0:T(8,128)(2,1)}, bf16[1,1,768,256]{2,3,1,0:T(8,128)(2,1)}, u32[]{:S(2)}, u32[]{:S(2)}) collective-permute-start(bf16[1,1,768,256]{2,3,1,0:T(8,128)(2,1)} %convert_bitcast_fusion.1), channel_id=1, source_target_pairs={{16,0},{32,16},{48,32},{64,48},{80,64},{96,80},{112,96},{17,1},{33... | collective-permute-start | bytes 1179656 | tf_op jit(solution)/shard_map/ppermute | solution.py:26
  300.9 48.4 %collective-permute-start.18 = (bf16[7,256,256]{1,2,0:T(8,128)(2,1)}, bf16[7,256,256]{1,2,0:T(8,128)(2,1)}, u32[]{:S(2)}, u32[]{:S(2)}) collective-permute-start(bf16[7,256,256]{1,2,0:T(8,128)(2,1)} %bitcast_dynamic-update-slice_fusion.25), channel_id=1, source_target_pairs={{0,16},{16,32},{32,48},{48,64},{64,80},{80,96},{96,112},{1,17},{17... | collective-permute-start | bytes 2752520 | tf_op jit(solution)/shard_map/ppermute | solution.py:15
  333.0 23.7 %collective-permute-start.19 = (bf16[7,256,256]{1,2,0:T(8,128)(2,1)}, bf16[7,256,256]{1,2,0:T(8,128)(2,1)S(1)}, u32[]{:S(2)}, u32[]{:S(2)}) collective-permute-start(bf16[7,256,256]{1,2,0:T(8,128)(2,1)} %bitcast_dynamic-update-slice_fusion.25), channel_id=1, source_target_pairs={{16,0},{32,16},{48,32},{64,48},{80,64},{96,80},{112,96},{17,1},{33... | collective-permute-start | bytes 2752520 | tf_op jit(solution)/shard_map/ppermute | solution.py:15
  334.9 25.7 %collective-permute-start.20 = (bf16[7,256,256]{1,2,0:T(8,128)(2,1)}, bf16[7,256,256]{1,2,0:T(8,128)(2,1)S(1)}, u32[]{:S(2)}, u32[]{:S(2)}) collective-permute-start(bf16[7,256,256]{1,2,0:T(8,128)(2,1)} %bitcast_dynamic-update-slice_fusion.25), channel_id=1, source_target_pairs={{32,0},{48,16},{64,32},{80,48},{96,64},{112,80},{33,1},{49,17},{65... | collective-permute-start | bytes 2752520 | tf_op jit(solution)/shard_map/ppermute | solution.py:15
  338.6 23.0 %collective-permute-start.21 = (bf16[7,256,256]{1,2,0:T(8,128)(2,1)}, bf16[7,256,256]{1,2,0:T(8,128)(2,1)S(1)}, u32[]{:S(2)}, u32[]{:S(2)}) collective-permute-start(bf16[7,256,256]{1,2,0:T(8,128)(2,1)} %bitcast_dynamic-update-slice_fusion.25), channel_id=1, source_target_pairs={{48,0},{64,16},{80,32},{96,48},{112,64},{49,1},{65,17},{81,33},{97... | collective-permute-start | bytes 2752520 | tf_op jit(solution)/shard_map/ppermute | solution.py:15
  342.0 45.4 %collective-permute-start.8 = (bf16[3,1,768,256]{2,3,1,0:T(8,128)(2,1)}, bf16[3,1,768,256]{2,3,1,0:T(8,128)(2,1)}, u32[]{:S(2)}, u32[]{:S(2)}) collective-permute-start(bf16[3,1,768,256]{2,3,1,0:T(8,128)(2,1)} %pad_maximum_fusion.2), channel_id=1, source_target_pairs={{0,1},{1,2},{2,3},{3,4},{4,5},{5,6},{6,7},{7,8},{8,9},{9,10},{10,1... | collective-permute-start | bytes 3538952 | tf_op jit(solution)/shard_map/ppermute | solution.py:23
  349.3 38.2 %collective-permute-start.9 = (bf16[3,1,768,256]{2,3,1,0:T(8,128)(2,1)}, bf16[3,1,768,256]{2,3,1,0:T(8,128)(2,1)}, u32[]{:S(2)}, u32[]{:S(2)}) collective-permute-start(bf16[3,1,768,256]{2,3,1,0:T(8,128)(2,1)} %pad_maximum_fusion.2), channel_id=1, source_target_pairs={{1,0},{2,1},{3,2},{4,3},{5,4},{6,5},{7,6},{8,7},{9,8},{10,9},{11,1... | collective-permute-start | bytes 3538952 | tf_op jit(solution)/shard_map/ppermute | solution.py:26
  403.3 330.8 %all-reduce.10.cloned.1.call-start = ((), (), s32[]{:S(2)}) async-start(), calls=%async_computation.1 | async-start | bytes 524288 | tf_op jit(solution)/shard_map/psum | solution.py:160
  595.0 588.9 %all-reduce.12.cloned.1.call-start = ((), (), s32[]{:S(2)}) async-start(), calls=%async_computation.2 | async-start | bytes 1048576 | tf_op jit(solution)/shard_map/psum | solution.py:158
  851.4 16.7 %collective-permute-start.30 = (bf16[256,256]{0,1:T(8,128)(2,1)S(1)}, bf16[256,256]{0,1:T(8,128)(2,1)S(1)}, u32[]{:S(2)}, u32[]{:S(2)}) collective-permute-start(bf16[256,256]{0,1:T(8,128)(2,1)S(1)} %bitcast.420), channel_id=1, source_target_pairs={{0,3},{1,4},{2,5},{3,6},{4,7},{5,8},{6,9},{7,10},{8,11},{9,12},{10... | collective-permute-start | bytes 393224 | tf_op jit(solution)/shard_map/ppermute | solution.py:15
  868.1 12.3 collective-permute-start.35
  881.1 52.9 %collective-permute-start.36 = (bf16[7,256,256]{1,2,0:T(8,128)(2,1)}, bf16[7,256,256]{1,2,0:T(8,128)(2,1)}, u32[]{:S(2)}, u32[]{:S(2)}) collective-permute-start(bf16[7,256,256]{1,2,0:T(8,128)(2,1)} %bitcast_dynamic-update-slice_fusion.19), channel_id=1, source_target_pairs={{0,48},{16,64},{32,80},{48,96},{64,112},{1,49},{17,65},{33,81},{49... | collective-permute-start | bytes 2752520 | tf_op jit(solution)/shard_map/ppermute | solution.py:15
  889.4 48.1 %collective-permute-start.37 = (bf16[7,256,256]{1,2,0:T(8,128)(2,1)}, bf16[7,256,256]{1,2,0:T(8,128)(2,1)}, u32[]{:S(2)}, u32[]{:S(2)}) collective-permute-start(bf16[7,256,256]{1,2,0:T(8,128)(2,1)} %bitcast_dynamic-update-slice_fusion.19), channel_id=1, source_target_pairs={{0,32},{16,48},{32,64},{48,80},{64,96},{80,112},{1,33},{17,49},{33... | collective-permute-start | bytes 2752520 | tf_op jit(solution)/shard_map/ppermute | solution.py:15
  891.6 38.0 %collective-permute-start.26 = (bf16[1,1,768,256]{2,3,1,0:T(8,128)(2,1)S(1)}, bf16[1,1,768,256]{2,3,1,0:T(8,128)(2,1)S(1)}, u32[]{:S(2)}, u32[]{:S(2)}) collective-permute-start(bf16[1,1,768,256]{2,3,1,0:T(8,128)(2,1)S(1)} %convert_bitcast_fusion), channel_id=1, source_target_pairs={{0,16},{16,32},{32,48},{48,64},{64,80},{80,96},{96,112},{1,17},{17... | collective-permute-start | bytes 1179656 | tf_op jit(solution)/shard_map/ppermute | solution.py:23
  893.5 38.0 %collective-permute-start.27 = (bf16[1,1,768,256]{2,3,1,0:T(8,128)(2,1)S(1)}, bf16[1,1,768,256]{2,3,1,0:T(8,128)(2,1)S(1)}, u32[]{:S(2)}, u32[]{:S(2)}) collective-permute-start(bf16[1,1,768,256]{2,3,1,0:T(8,128)(2,1)S(1)} %convert_bitcast_fusion), channel_id=1, source_target_pairs={{16,0},{32,16},{48,32},{64,48},{80,64},{96,80},{112,96},{17,1},{33... | collective-permute-start | bytes 1179656 | tf_op jit(solution)/shard_map/ppermute | solution.py:26
  896.0 48.7 %collective-permute-start.38 = (bf16[7,256,256]{1,2,0:T(8,128)(2,1)}, bf16[7,256,256]{1,2,0:T(8,128)(2,1)}, u32[]{:S(2)}, u32[]{:S(2)}) collective-permute-start(bf16[7,256,256]{1,2,0:T(8,128)(2,1)} %bitcast_dynamic-update-slice_fusion.19), channel_id=1, source_target_pairs={{0,16},{16,32},{32,48},{48,64},{64,80},{80,96},{96,112},{1,17},{17... | collective-permute-start | bytes 2752520 | tf_op jit(solution)/shard_map/ppermute | solution.py:15
  929.6 23.7 %collective-permute-start.39 = (bf16[7,256,256]{1,2,0:T(8,128)(2,1)}, bf16[7,256,256]{1,2,0:T(8,128)(2,1)S(1)}, u32[]{:S(2)}, u32[]{:S(2)}) collective-permute-start(bf16[7,256,256]{1,2,0:T(8,128)(2,1)} %bitcast_dynamic-update-slice_fusion.19), channel_id=1, source_target_pairs={{16,0},{32,16},{48,32},{64,48},{80,64},{96,80},{112,96},{17,1},{33... | collective-permute-start | bytes 2752520 | tf_op jit(solution)/shard_map/ppermute | solution.py:15
  931.5 25.7 %collective-permute-start.40 = (bf16[7,256,256]{1,2,0:T(8,128)(2,1)}, bf16[7,256,256]{1,2,0:T(8,128)(2,1)S(1)}, u32[]{:S(2)}, u32[]{:S(2)}) collective-permute-start(bf16[7,256,256]{1,2,0:T(8,128)(2,1)} %bitcast_dynamic-update-slice_fusion.19), channel_id=1, source_target_pairs={{32,0},{48,16},{64,32},{80,48},{96,64},{112,80},{33,1},{49,17},{65... | collective-permute-start | bytes 2752520 | tf_op jit(solution)/shard_map/ppermute | solution.py:15
  934.0 24.2 %collective-permute-start.41 = (bf16[7,256,256]{1,2,0:T(8,128)(2,1)}, bf16[7,256,256]{1,2,0:T(8,128)(2,1)S(1)}, u32[]{:S(2)}, u32[]{:S(2)}) collective-permute-start(bf16[7,256,256]{1,2,0:T(8,128)(2,1)} %bitcast_dynamic-update-slice_fusion.19), channel_id=1, source_target_pairs={{48,0},{64,16},{80,32},{96,48},{112,64},{49,1},{65,17},{81,33},{97... | collective-permute-start | bytes 2752520 | tf_op jit(solution)/shard_map/ppermute | solution.py:15
  937.4 44.0 %collective-permute-start.28 = (bf16[3,1,768,256]{2,3,1,0:T(8,128)(2,1)}, bf16[3,1,768,256]{2,3,1,0:T(8,128)(2,1)}, u32[]{:S(2)}, u32[]{:S(2)}) collective-permute-start(bf16[3,1,768,256]{2,3,1,0:T(8,128)(2,1)} %pad_maximum_fusion.3), channel_id=1, source_target_pairs={{0,1},{1,2},{2,3},{3,4},{4,5},{5,6},{6,7},{7,8},{8,9},{9,10},{10,1... | collective-permute-start | bytes 3538952 | tf_op jit(solution)/shard_map/ppermute | solution.py:23
  944.7 36.7 %collective-permute-start.29 = (bf16[3,1,768,256]{2,3,1,0:T(8,128)(2,1)}, bf16[3,1,768,256]{2,3,1,0:T(8,128)(2,1)}, u32[]{:S(2)}, u32[]{:S(2)}) collective-permute-start(bf16[3,1,768,256]{2,3,1,0:T(8,128)(2,1)} %pad_maximum_fusion.3), channel_id=1, source_target_pairs={{1,0},{2,1},{3,2},{4,3},{5,4},{6,5},{7,6},{8,7},{9,8},{10,9},{11,1... | collective-permute-start | bytes 3538952 | tf_op jit(solution)/shard_map/ppermute | solution.py:26
  996.7 332.6 %all-reduce.14.cloned.1.call-start = ((), (), s32[]{:S(2)}) async-start(), calls=%async_computation.3 | async-start | bytes 524288 | tf_op jit(solution)/shard_map/psum | solution.py:160
  (60 other events, 1465.7 us)
Sparse Core Ops, SparseCore 0:
  10.5 110.3 all-gather.2
  403.4 186.7 all-reduce.7
  595.1 138.9 all-reduce.9
  996.8 186.9 all-reduce.11
  1189.2 140.1 all-reduce.13
